TPU v7x, 32 devices: a whole 2x2x4 slice. The times are simulated.
32 devices in a mesh: dp: 4 (over y, x), mp: 8 (over z, core).
Axes of the slice: x: 2, y: 2, z: 4, core: 2. Of those that a mesh axis runs over, the one named last changes fastest.
Arguments:
- activations: bfloat16 [4096, 2048], P('dp', 'mp'), may hold values from -6 to 6
- out_grad: bfloat16 [4096, 8192], P('dp'), may hold values from -0.8984375 to 0.8984375
- old_weight: bfloat16 [8, 256, 8192], P('mp', 'dp'), may hold values from -0.125 to 0.125
- old_first: float32 [8, 256, 8192], P('mp', 'dp'), may hold values from -6 to 6
- old_second: float32 [8, 256, 8192], P('mp', 'dp'), may hold values from 0.25 to 4
- step: int32 [1], replicated, may hold values from 1 to 31
- next_input: bfloat16 [4096, 2048], P('dp', 'mp'), may hold values from -6 to 6
Outputs:
- new_weight: bfloat16 [8, 344, 8192], P('mp', 'dp')
- new_first: float32 [8, 344, 8192], P('mp', 'dp')
- new_second: float32 [8, 344, 8192], P('mp', 'dp')
- output: bfloat16 [4096, 8192], P('dp', 'mp')
Inputs may be any that keep to these rules, and one draw needn't show every extreme that they name: `step`: the number of Adam steps taken, this one included.
All inputs are finite; a program needn't handle non-finite values.
Results may differ from a plain program's by a relative error of at most 0.0049.
Values may be sent and summed in bfloat16 or wider, within the bound.
A program may use at most 192 MiB of HBM per device.

v0:
```python
import jax
import jax.numpy as jnp
from jax import lax
from jax.sharding import PartitionSpec as P


def from_behind(block, axis, distance):
    devices = range(lax.axis_size(axis))
    route = [(i - distance, i) for i in devices if i - distance in devices]
    return lax.ppermute(block, axis, route)


def body(activations, out_grad, old_weight, old_first, old_second, step, next_input):
    owners = lax.axis_size("dp")
    owner = lax.axis_index("dp")
    old_rows = old_weight.shape[1]
    width = old_weight.shape[2]
    held_rows = old_rows * owners
    shard_rows = (held_rows + owners - 2) // (owners - 1)
    padded_rows = owners * shard_rows
    tok_rows = activations.shape[0]
    moments = jnp.stack([old_first[0], old_second[0]])
    weight_next = from_behind(old_weight[0], "dp", -1)
    moment_next = from_behind(moments, "dp", -1)
    weight_rows = jnp.concatenate(
        [old_weight[0], weight_next, jnp.zeros((shard_rows, width), jnp.bfloat16)], 0
    )
    moment_rows = jnp.concatenate(
        [moments, moment_next, jnp.zeros((2, shard_rows, width), jnp.float32)], 1
    )
    begin = owner * (shard_rows - old_rows)
    weight_mine = lax.dynamic_slice_in_dim(weight_rows, begin, shard_rows, 0)
    moment_mine = lax.dynamic_slice_in_dim(moment_rows, begin, shard_rows, 1)
    row_index = owner * shard_rows + lax.broadcasted_iota(jnp.int32, (shard_rows, 1), 0)
    valid = row_index < held_rows
    feat_pad = jnp.concatenate(
        [activations, jnp.zeros((tok_rows, padded_rows - held_rows), jnp.bfloat16)], 1
    )
    grad = lax.psum_scatter(
        lax.dot_general(
            feat_pad, out_grad, (((0,), (0,)), ((), ())), preferred_element_type=jnp.float32
        ),
        "dp",
        scatter_dimension=0,
        tiled=True,
    )
    step_float = step[0].astype(jnp.float32)
    first_fix = 1.0 - jnp.power(jnp.float32(0.9), step_float)
    second_fix = 1.0 - jnp.power(jnp.float32(0.95), step_float)
    new_first = 0.9 * moment_mine[0] + 0.1 * grad
    new_second = 0.95 * moment_mine[1] + 0.05 * grad * grad
    safe_second = jnp.where(valid, new_second, jnp.float32(1.0))
    update = new_first / first_fix / (jnp.sqrt(safe_second / second_fix) + 1e-08)
    update = jnp.where(valid, update, jnp.float32(0.0))
    new_weight = (weight_mine.astype(jnp.float32) - 0.01 * update).astype(jnp.bfloat16)
    weight_all_new = lax.all_gather(new_weight, "dp", axis=0, tiled=True)[:held_rows]
    weight_cols = lax.all_to_all(weight_all_new, "mp", split_axis=1, concat_axis=0, tiled=True)
    input_all = lax.all_gather(next_input, "mp", axis=1, tiled=True)
    output = jnp.dot(input_all, weight_cols, preferred_element_type=jnp.float32).astype(
        jnp.bfloat16
    )
    return (new_weight[None], new_first[None], new_second[None], output)


def solution(mesh):
    return jax.shard_map(
        body,
        mesh=mesh,
        in_specs=(
            P("dp", "mp"),
            P("dp", None),
            P("mp", "dp", None),
            P("mp", "dp", None),
            P("mp", "dp", None),
            P(),
            P("dp", "mp"),
        ),
        out_specs=(P("mp", "dp", None), P("mp", "dp", None), P("mp", "dp", None), P("dp", "mp")),
        check_vma=False,
    )
```

profile of v0, /device:TPU:0, one launch (start us, length us, event | category | flops | bytes accessed | tf_op | source)
XLA Modules:
  0.0 492.6 jit_solution(16472965787498967166)
XLA Ops:
  7.2 0.0 copy-start.1
  7.2 0.0 all-gather.6.cloned.1.call-start
  7.2 3.2 constant_dynamic-update-slice_fusion.1
  10.4 0.0 copy-done.1
  10.4 0.0 copy-start.3
  10.4 1.5 constant_dynamic-update-slice_fusion
  11.9 1.3 collective-permute-start.1
  13.2 0.0 copy-done.3
  13.2 12.2 %fusion.10 = f32[344,8192]{1,0:T(8,128)} fusion(bf16[1024,8192]{1,0:T(8,128)(2,1)} %param.8, bf16[1024,256]{1,0:T(8,128)(2,1)S(1)} %copy-done.3), kind=kOutput, calls=%fused_computation.19 | convolution fusion | flops 5771362304 | bytes 28573696 | tf_op jit(solution)/shard_map/dot_general | solution.py:40
  25.4 0.0 copy-start.4
  25.4 190.4 %fusion = f32[96,8192]{1,0:T(8,128)S(1)} fusion(f32[344,8192]{1,0:T(8,128)} %fusion.10), kind=kCustom, calls=%all-reduce-scatter | all-reduce-scatter fusion | flops 3145729 | bytes 14418432
  215.8 1.0 slice.15
  216.8 4.7 collective-permute-start.2
  221.5 1.3 collective-permute-start
  223.5 0.0 copy-done.4
  223.5 0.6 dynamic-slice.6
  224.8 0.1 pad_dynamic-slice_fusion.4
  224.9 0.1 pad_dynamic-slice_fusion.5
  225.0 17.6 %collective-permute-done.2 = f32[30,8192]{1,0:T(8,128)} collective-permute-done((f32[30,8192]{1,0:T(8,128)}, f32[30,8192]{1,0:T(8,128)}, u32[]{:S(2)}, u32[]{:S(2)}) %collective-permute-start.2) | collective-permute-done | bytes 983072
  242.6 12.3 %concatenate.12 = f32[126,8192]{1,0:T(8,128)} concatenate(f32[30,8192]{1,0:T(8,128)} %collective-permute-done.2, f32[96,8192]{1,0:T(8,128)S(1)} %fusion), dimensions={0} | concatenate | bytes 8257536
  254.9 0.0 copy-start
  254.9 0.0 copy-start.2
  254.9 0.0 collective-permute-done.1
  254.9 4.4 fusion.2
  259.3 7.7 %collective-permute-done = bf16[64,8192]{1,0:T(8,128)(2,1)} collective-permute-done((bf16[64,8192]{1,0:T(8,128)(2,1)}, bf16[64,8192]{1,0:T(8,128)(2,1)}, u32[]{:S(2)}, u32[]{:S(2)}) %collective-permute-start) | collective-permute-done | bytes 1048608 | tf_op jit(solution)/shard_map/ppermute | solution.py:10
  267.0 0.0 copy-done
  267.0 0.0 copy-done.2
  267.0 5.9 %fusion.13 = (f32[1,86,8192]{2,1,0:T(8,128)S(1)}, f32[1,86,8192]{2,1,0:T(8,128)}, bf16[1,86,8192]{2,1,0:T(8,128)(2,1)}) fusion(f32[126,8192]{1,0:T(8,128)S(1)} %copy-done, u32[]{:S(6)} %subtract, f32[2,86,8192]{2,1,0:T(8,128)S(1)} %fusion.2, f32[]{:T(128)} %bitcast.4, f32[]{:T(128)} %bitcast.2, pred[86]{0:T(512)(128)(4,1)S(1)} %add_compare_fusion, ...), kind=kLoop, calls=%fused_computation.22 | loop fusion | flops 15499264 | bytes 17596690 | tf_op jit(solution)/shard_map/broadcast_in_dim | solution.py:62
  272.9 0.0 all-gather.6.cloned.1.call-update
  272.9 0.0 all-gather.4.cloned.1.call-start
  272.9 0.7 all-gather.4.cloned.1.call-update
  273.6 64.6 %all-gather.6.cloned.1.call-done = bf16[4,86,8192]{2,1,0:T(8,128)(2,1)} async-done(((bf16[1,86,8192]{2,1,0:T(8,128)(2,1)}), bf16[4,86,8192]{2,1,0:T(8,128)(2,1)}) %all-gather.6.cloned.1.call-update) | async-done | bytes 5636112 | tf_op jit(solution)/shard_map/all_gather | solution.py:56
  338.2 6.9 %reshape.32 = bf16[344,8192]{1,0:T(8,128)(2,1)} reshape(bf16[4,86,8192]{2,1,0:T(8,128)(2,1)} %all-gather.6.cloned.1.call-done) | data formatting | bytes 11272192
  345.1 0.0 slice-start
  345.1 2.4 slice-done
  347.5 2.4 copy.24
  349.9 4.7 all-to-all-start
  354.7 6.3 %copy.19 = f32[1,86,8192]{2,0,1:T(1,128)} copy(f32[1,86,8192]{2,1,0:T(8,128)} %get-tuple-element.17) | data formatting | bytes 5636096
  361.0 4.5 copy.20
  365.4 57.2 %all-gather.4.cloned.1.call-done = bf16[1024,2048]{1,0:T(8,128)(2,1)} async-done(((bf16[1024,256]{1,0:T(8,128)(2,1)}), bf16[1024,2048]{1,0:T(8,128)(2,1)}) %all-gather.4.cloned.1.call-update) | async-done | bytes 4194320 | tf_op jit(solution)/shard_map/all_gather | solution.py:58
  422.7 52.5 %all-to-all-done = bf16[256,8,1024]{2,0,1:T(8,128)(2,1)} async-done(((bf16[256,8,1024]{2,0,1:T(8,128)(2,1)}), bf16[256,8,1024]{2,0,1:T(8,128)(2,1)}, u32[]{:S(2)}, u32[]{:S(2)}) %all-to-all-start) | async-done | bytes 4194336 | tf_op jit(solution)/shard_map/all_to_all | solution.py:57
  475.2 8.0 %convert_bitcast_fusion = bf16[1024,1024]{0,1:T(8,128)(2,1)S(1)} fusion(bf16[2048,1024]{1,0:T(8,128)(2,1)} %bitcast.9, bf16[1024,2048]{1,0:T(8,128)(2,1)} %all-gather.4.cloned.1.call-done), kind=kOutput, calls=%fused_computation.15 | convolution fusion | flops 4296015872 | bytes 10485760 | tf_op jit(solution)/shard_map/dot_general | solution.py:59
  483.2 2.6 copy.21
  (3 shorter events, 0.0 us)
Async XLA Ops:
  7.2 3.2 copy-start.1
  7.2 331.0 %all-gather.6.cloned.1.call-start = ((), (), s32[]{:S(2)}) async-start(), calls=%async_computation.2 | async-start | bytes 7208960 | tf_op jit(solution)/shard_map/all_gather | solution.py:56
  10.4 2.8 copy-start.3
  11.9 243.0 %collective-permute-start.1 = (f32[2,64,8192]{2,1,0:T(8,128)}, f32[2,64,8192]{2,1,0:T(8,128)}, u32[]{:S(2)}, u32[]{:S(2)}) collective-permute-start(f32[2,64,8192]{2,1,0:T(8,128)} %constant_dynamic-update-slice_fusion), channel_id=1, source_target_pairs={{8,0},{16,8},{24,16},{9,1},{17,9},{25,17},{10,2},{18,10},{26,18},{... | collective-permute-start | bytes 12582920 | tf_op jit(solution)/shard_map/ppermute | solution.py:10
  25.4 198.2 %copy-start.4 = (u32[32]{0:T(128)S(1)}, u32[32]{0:T(128)}, u32[]{:S(2)}) copy-start(u32[32]{0:T(128)} %constant.51) | copy-start | bytes 388
  216.8 25.7 %collective-permute-start.2 = (f32[30,8192]{1,0:T(8,128)}, f32[30,8192]{1,0:T(8,128)}, u32[]{:S(2)}, u32[]{:S(2)}) collective-permute-start(f32[30,8192]{1,0:T(8,128)} %slice.15), channel_id=1, source_target_pairs={{0,8},{8,16},{16,24},{1,9},{9,17},{17,25},{2,10},{10,18},{18,26},{... | collective-permute-start | bytes 2949128
  221.5 45.5 %collective-permute-start = (bf16[64,8192]{1,0:T(8,128)(2,1)}, bf16[64,8192]{1,0:T(8,128)(2,1)}, u32[]{:S(2)}, u32[]{:S(2)}) collective-permute-start(bf16[64,8192]{1,0:T(8,128)(2,1)} %bitcast.42), channel_id=1, source_target_pairs={{8,0},{16,8},{24,16},{9,1},{17,9},{25,17},{10,2},{18,10},{26,18},{... | collective-permute-start | bytes 3145736 | tf_op jit(solution)/shard_map/ppermute | solution.py:10
  254.9 12.1 %copy-start = (f32[126,8192]{1,0:T(8,128)S(1)}, f32[126,8192]{1,0:T(8,128)}, u32[]{:S(2)}) copy-start(f32[126,8192]{1,0:T(8,128)} %concatenate.12) | copy-start | bytes 12386308
  254.9 12.1 %copy-start.2 = (bf16[1,64,8192]{2,1,0:T(8,128)(2,1)S(1)}, bf16[1,64,8192]{2,1,0:T(8,128)(2,1)}, u32[]{:S(2)}) copy-start(bf16[1,64,8192]{2,1,0:T(8,128)(2,1)} %param.9) | copy-start | bytes 3145732
  272.9 149.8 %all-gather.4.cloned.1.call-start = ((), (), s32[]{:S(2)}) async-start(), calls=%async_computation.1 | async-start | bytes 4718592 | tf_op jit(solution)/shard_map/all_gather | solution.py:58
  345.1 2.4 slice-start
  349.9 125.3 %all-to-all-start = ((bf16[256,8,1024]{2,0,1:T(8,128)(2,1)}), bf16[256,8,1024]{2,0,1:T(8,128)(2,1)}, u32[]{:S(2)}, u32[]{:S(2)}) async-start(bf16[256,8,1024]{2,0,1:T(8,128)(2,1)} %bitcast.41), calls=%async_computation | async-start | bytes 8388608 | tf_op jit(solution)/shard_map/all_to_all | solution.py:57
Sparse Core Ops, SparseCore 0:
  273.0 65.1 all-gather.5
  339.8 82.8 all-gather.3
where the time goes:
time: 494 us; the launch traced here: 493 us
  waiting for transfers between devices  200 us (40%)
  blocking collectives  190 us (38%)
  local copies, waits for them, and re-layouts  43.9 us (9%)
  matrix products  20.2 us (4%)
  between operations  15.5 us (3%)
  starting transfers between devices  12 us (2%)
  other arithmetic  10.3 us (2%)
    unnamed x1, blocking collectives  190 us
    all_gather x1, waiting for transfers between devices, body(): lax.all_gather(new_weight, 'dp', axis=0, tiled=True)[:held_rows]  64.6 us
    all_gather x1, waiting for transfers between devices, body(): input_all = lax.all_gather(next_input, 'mp', axis=1, tiled=True)  57.2 us
    all_to_all x1, waiting for transfers between devices, body(): lax.all_to_all(weight_all_new, 'mp', split_axis=1, concat_axis=0, tiled=T...  52.5 us
    unnamed x18, local copies, waits for them, and re-layouts  37.4 us
    unnamed x3, waiting for transfers between devices  18.3 us
    dot_general x1, matrix products, body(): lax.dot_general(feat_pad, out_grad, (((0,), (0,)), ((), ())), preferred_e...  12.2 us
  transfers between devices with their start and end apart: 6, of which 5 were waited for; matrix products, arithmetic and copies ran while one was open for 49% of the time, Pallas kernels for 0%

commit v1 on v0

--- a/solution.py
+++ b/solution.py
@@ -55,7 +55,12 @@
     new_weight = (weight_mine.astype(jnp.float32) - 0.01 * update).astype(jnp.bfloat16)
     weight_all_new = lax.all_gather(new_weight, "dp", axis=0, tiled=True)[:held_rows]
     weight_cols = lax.all_to_all(weight_all_new, "mp", split_axis=1, concat_axis=0, tiled=True)
-    input_all = lax.all_gather(next_input, "mp", axis=1, tiled=True)
+    ring = [next_input]
+    for hop in range(7):
+        ring.append(lax.ppermute(ring[-1], "mp", [(dev, (dev + 1) % 8) for dev in range(8)]))
+    input_all = jnp.roll(
+        jnp.concatenate(ring[::-1], axis=1), (lax.axis_index("mp") + 1) * ring[0].shape[1], axis=1
+    )
     output = jnp.dot(input_all, weight_cols, preferred_element_type=jnp.float32).astype(
         jnp.bfloat16
     )

time: 494 us -> 541 us (1.095); the launches traced: 493 us -> 533 us
  starting transfers between devices: 12 us -> 28.4 us
  waiting for transfers between devices: 200 us -> 216 us
  local copies, waits for them, and re-layouts: 43.9 us -> 50.6 us
    ppermute x0 -> x7, waiting for transfers between devices: none -> 125 us  [body(): lax.ppermute(ring[-1], 'mp', [(dev, (dev + 1) % 8) for dev in range(8)])]
    all_gather x1 -> x0, waiting for transfers between devices: 57.2 us -> none  [body(): input_all = lax.all_gather(next_input, 'mp', axis=1, tiled=True)]
    all_to_all x1, waiting for transfers between devices: 52.5 us -> 0.01 us  [body(): lax.all_to_all(weight_all_new, 'mp', split_axis=1, concat_axis=0, tiled=T...]
    ppermute x0 -> x7, starting transfers between devices: none -> 16.4 us  [body(): lax.ppermute(ring[-1], 'mp', [(dev, (dev + 1) % 8) for dev in range(8)])]
    unnamed x18 -> x58, local copies, waits for them, and re-layouts: 37.4 us -> 44.4 us
    unnamed x3 -> x2, waiting for transfers between devices: 18.3 us -> 17.6 us
  transfers between devices with their start and end apart: 6 -> 12, of which waited for: 5 -> 10; matrix products, arithmetic and copies ran while one was open for 49% -> 45% of each run, Pallas kernels for 0% -> 0%
where the time goes in v1:
time: 541 us; the launch traced here: 533 us
  waiting for transfers between devices  216 us (40%)
  blocking collectives  190 us (35%)
  local copies, waits for them, and re-layouts  50.6 us (9%)
  starting transfers between devices  28.4 us (5%)
  matrix products  21.4 us (4%)
  between operations  15.7 us (3%)
  other arithmetic  10.3 us (2%)
    unnamed x1, blocking collectives  190 us
    ppermute x7, waiting for transfers between devices, body(): lax.ppermute(ring[-1], 'mp', [(dev, (dev + 1) % 8) for dev in range(8)])  125 us
    all_gather x1, waiting for transfers between devices, body(): lax.all_gather(new_weight, 'dp', axis=0, tiled=True)[:held_rows]  65.3 us
    unnamed x58, local copies, waits for them, and re-layouts  44.4 us
    unnamed x2, waiting for transfers between devices  17.6 us
    ppermute x7, starting transfers between devices, body(): lax.ppermute(ring[-1], 'mp', [(dev, (dev + 1) % 8) for dev in range(8)])  16.4 us
    dot_general x1, matrix products, body(): lax.dot_general(feat_pad, out_grad, (((0,), (0,)), ((), ())), preferred_e...  12.2 us
  transfers between devices with their start and end apart: 12, of which 10 were waited for; matrix products, arithmetic and copies ran while one was open for 45% of the time, Pallas kernels for 0%

profile of v1, /device:TPU:0, one launch (start us, length us, event | category | flops | bytes accessed | tf_op | source)
XLA Modules:
  0.0 532.6 jit_solution(16846602032928018533)
XLA Ops:
  7.2 0.0 all-gather.3.cloned.1.call-start
  7.2 3.2 constant_dynamic-update-slice_fusion.1
  10.4 1.5 constant_dynamic-update-slice_fusion
  11.9 1.3 collective-permute-start.1
  13.2 12.2 %fusion.15 = f32[344,8192]{1,0:T(8,128)} fusion(bf16[1024,8192]{1,0:T(8,128)(2,1)} %param.8, bf16[1024,256]{1,0:T(8,128)(2,1)S(1)} %copy-done.15), kind=kOutput, calls=%fused_computation.21 | convolution fusion | flops 5771362304 | bytes 28573696 | tf_op jit(solution)/shard_map/dot_general | solution.py:40
  25.4 190.4 %fusion = f32[96,8192]{1,0:T(8,128)S(1)} fusion(f32[344,8192]{1,0:T(8,128)} %fusion.15), kind=kCustom, calls=%all-reduce-scatter | all-reduce-scatter fusion | flops 3145729 | bytes 14418432
  215.8 1.0 slice.15
  216.8 4.7 collective-permute-start.9
  221.5 1.3 collective-permute-start
  223.5 0.6 dynamic-slice.6
  224.8 0.1 pad_dynamic-slice_fusion.4
  224.9 0.1 pad_dynamic-slice_fusion.5
  224.9 17.6 %collective-permute-done.9 = f32[30,8192]{1,0:T(8,128)} collective-permute-done((f32[30,8192]{1,0:T(8,128)}, f32[30,8192]{1,0:T(8,128)}, u32[]{:S(2)}, u32[]{:S(2)}) %collective-permute-start.9) | collective-permute-done | bytes 983072
  242.6 12.2 %concatenate.19 = f32[126,8192]{1,0:T(8,128)} concatenate(f32[30,8192]{1,0:T(8,128)} %collective-permute-done.9, f32[96,8192]{1,0:T(8,128)S(1)} %fusion), dimensions={0} | concatenate | bytes 8257536
  254.8 0.0 collective-permute-done.1
  254.8 4.4 fusion.2
  259.1 7.8 %collective-permute-done = bf16[64,8192]{1,0:T(8,128)(2,1)} collective-permute-done((bf16[64,8192]{1,0:T(8,128)(2,1)}, bf16[64,8192]{1,0:T(8,128)(2,1)}, u32[]{:S(2)}, u32[]{:S(2)}) %collective-permute-start) | collective-permute-done | bytes 1048608 | tf_op jit(solution)/shard_map/ppermute | solution.py:10
  267.0 5.9 %fusion.18 = (f32[1,86,8192]{2,1,0:T(8,128)S(1)}, f32[1,86,8192]{2,1,0:T(8,128)}, bf16[1,86,8192]{2,1,0:T(8,128)(2,1)}) fusion(f32[126,8192]{1,0:T(8,128)S(1)} %copy-done, u32[]{:S(6)} %subtract.1, f32[2,86,8192]{2,1,0:T(8,128)S(1)} %fusion.2, f32[]{:T(128)} %bitcast.4, f32[]{:T(128)} %bitcast.2, pred[86]{0:T(512)(128)(4,1)S(1)} %add_compare_fusion, ...), kind=kLoop, calls=%fused_computation.24 | loop fusion | flops 15499264 | bytes 17596690 | tf_op jit(solution)/shard_map/broadcast_in_dim | solution.py:67
  272.9 0.0 all-gather.3.cloned.1.call-update
  272.9 65.3 %all-gather.3.cloned.1.call-done = bf16[4,86,8192]{2,1,0:T(8,128)(2,1)} async-done(((bf16[1,86,8192]{2,1,0:T(8,128)(2,1)}), bf16[4,86,8192]{2,1,0:T(8,128)(2,1)}) %all-gather.3.cloned.1.call-update) | async-done | bytes 5636112 | tf_op jit(solution)/shard_map/all_gather | solution.py:56
  338.2 6.9 %reshape.32 = bf16[344,8192]{1,0:T(8,128)(2,1)} reshape(bf16[4,86,8192]{2,1,0:T(8,128)(2,1)} %all-gather.3.cloned.1.call-done) | data formatting | bytes 11272192
  345.1 2.2 slice-done
  347.3 2.4 copy.21
  349.6 4.7 all-to-all-start
  354.4 0.5 collective-permute-start.2
  354.9 77.7 %collective-permute-done.2 = bf16[1024,256]{1,0:T(8,128)(2,1)S(1)} collective-permute-done((bf16[1024,256]{1,0:T(8,128)(2,1)S(1)}, bf16[1024,256]{1,0:T(8,128)(2,1)S(1)}, u32[]{:S(2)}, u32[]{:S(2)}) %collective-permute-start.2) | collective-permute-done | bytes 524320 | tf_op jit(solution)/shard_map/ppermute | solution.py:60
  432.6 0.8 copy-done.4
  433.4 0.0 collective-permute-start.3
  433.4 10.5 %collective-permute-done.3 = bf16[1024,256]{1,0:T(8,128)(2,1)S(1)} collective-permute-done((bf16[1024,256]{1,0:T(8,128)(2,1)S(1)}, bf16[1024,256]{1,0:T(8,128)(2,1)S(1)}, u32[]{:S(2)}, u32[]{:S(2)}) %collective-permute-start.3) | collective-permute-done | bytes 524320 | tf_op jit(solution)/shard_map/ppermute | solution.py:60
  443.9 0.8 copy-done.6
  444.7 10.5 %collective-permute-done.4 = bf16[1024,256]{1,0:T(8,128)(2,1)S(1)} collective-permute-done((bf16[1024,256]{1,0:T(8,128)(2,1)S(1)}, bf16[1024,256]{1,0:T(8,128)(2,1)S(1)}, u32[]{:S(2)}, u32[]{:S(2)}) %collective-permute-start.4) | collective-permute-done | bytes 524320 | tf_op jit(solution)/shard_map/ppermute | solution.py:60
  455.2 0.8 copy-done.8
  456.0 6.8 %collective-permute-start.5 = (bf16[1024,256]{1,0:T(8,128)(2,1)S(1)}, bf16[1024,256]{1,0:T(8,128)(2,1)S(1)}, u32[]{:S(2)}, u32[]{:S(2)}) collective-permute-start(bf16[1024,256]{1,0:T(8,128)(2,1)S(1)} %collective-permute-done.4), channel_id=1, source_target_pairs={{0,1},{1,2},{2,3},{3,4},{4,5},{5,6},{6,7},{7,0},{8,9},{9,10},{10,1... | collective-permute-start | bytes 1572872 | tf_op jit(solution)/shard_map/ppermute | solution.py:60
  462.7 3.7 collective-permute-done.5
  466.5 0.8 copy-done.10
  467.3 4.9 collective-permute-start.6
  472.1 5.5 %collective-permute-done.6 = bf16[1024,256]{1,0:T(8,128)(2,1)S(1)} collective-permute-done((bf16[1024,256]{1,0:T(8,128)(2,1)S(1)}, bf16[1024,256]{1,0:T(8,128)(2,1)S(1)}, u32[]{:S(2)}, u32[]{:S(2)}) %collective-permute-start.6) | collective-permute-done | bytes 524320 | tf_op jit(solution)/shard_map/ppermute | solution.py:60
  477.7 0.8 copy-done.12
  478.5 3.1 collective-permute-start.7
  481.5 7.4 %collective-permute-done.7 = bf16[1024,256]{1,0:T(8,128)(2,1)} collective-permute-done((bf16[1024,256]{1,0:T(8,128)(2,1)S(1)}, bf16[1024,256]{1,0:T(8,128)(2,1)}, u32[]{:S(2)}, u32[]{:S(2)}) %collective-permute-start.7) | collective-permute-done | bytes 524320 | tf_op jit(solution)/shard_map/ppermute | solution.py:60
  489.0 1.2 collective-permute-start.8
  490.2 9.5 %collective-permute-done.8 = bf16[1024,256]{1,0:T(8,128)(2,1)} collective-permute-done((bf16[1024,256]{1,0:T(8,128)(2,1)}, bf16[1024,256]{1,0:T(8,128)(2,1)}, u32[]{:S(2)}, u32[]{:S(2)}) %collective-permute-start.8) | collective-permute-done | bytes 524320 | tf_op jit(solution)/shard_map/ppermute | solution.py:60
  499.7 1.1 constant_dynamic-update-slice_fusion.17
  500.8 1.1 constant_dynamic-update-slice_fusion.16
  501.9 0.0 copy-start.13
  501.9 1.2 constant_dynamic-update-slice_fusion.15
  503.1 0.0 copy-start.11
  503.1 1.2 constant_dynamic-update-slice_fusion.14
  504.3 0.1 constant_dynamic-update-slice_fusion.13
  504.4 0.1 constant_dynamic-update-slice_fusion.12
  504.5 0.1 constant_dynamic-update-slice_fusion.11
  504.5 0.1 constant_dynamic-update-slice_fusion.10
  504.6 1.3 constant_dynamic-update-slice_fusion.9
  505.9 1.1 constant_dynamic-update-slice_fusion.8
  507.0 0.1 constant_dynamic-update-slice_fusion.7
  507.1 0.1 constant_dynamic-update-slice_fusion.6
  507.1 0.1 constant_dynamic-update-slice_fusion.5
  507.2 0.1 constant_dynamic-update-slice_fusion.4
  507.3 0.1 constant_dynamic-update-slice_fusion.3
  507.4 0.1 constant_dynamic-update-slice_fusion.2
  507.5 4.5 copy.17
  512.0 4.5 copy.18
  516.4 0.0 all-to-all-done
  516.4 9.3 %fusion.9 = bf16[1024,1024]{1,0:T(8,128)(2,1)} fusion(bf16[2048,1024]{1,0:T(8,128)(2,1)} %bitcast.9, bf16[1024,4096]{1,0:T(8,128)(2,1)} %copy-done.16, s32[]{:T(128)S(6)} %select_n.28), kind=kOutput, calls=%fused_computation.17 | convolution fusion | flops 4296015872 | bytes 10485764 | tf_op jit(solution)/shard_map/dot_general | solution.py:64
  (34 shorter events, 0.1 us)
Async XLA Ops:
  7.2 3.3 copy-start.2
  7.2 6.0 %copy-start.15 = (bf16[1024,256]{1,0:T(8,128)(2,1)S(1)}, bf16[1024,256]{1,0:T(8,128)(2,1)}, u32[]{:S(2)}) copy-start(bf16[1024,256]{1,0:T(8,128)(2,1)} %param.7) | copy-start | bytes 1572868
  7.2 331.0 %all-gather.3.cloned.1.call-start = ((), (), s32[]{:S(2)}) async-start(), calls=%async_computation.1 | async-start | bytes 7208960 | tf_op jit(solution)/shard_map/all_gather | solution.py:56
  11.9 242.9 %collective-permute-start.1 = (f32[2,64,8192]{2,1,0:T(8,128)}, f32[2,64,8192]{2,1,0:T(8,128)}, u32[]{:S(2)}, u32[]{:S(2)}) collective-permute-start(f32[2,64,8192]{2,1,0:T(8,128)} %constant_dynamic-update-slice_fusion), channel_id=1, source_target_pairs={{8,0},{16,8},{24,16},{9,1},{17,9},{25,17},{10,2},{18,10},{26,18},{... | collective-permute-start | bytes 12582920 | tf_op jit(solution)/shard_map/ppermute | solution.py:10
  25.4 198.2 %copy-start.17 = (u32[32]{0:T(128)S(1)}, u32[32]{0:T(128)}, u32[]{:S(2)}) copy-start(u32[32]{0:T(128)} %constant.78) | copy-start | bytes 388
  216.8 25.7 %collective-permute-start.9 = (f32[30,8192]{1,0:T(8,128)}, f32[30,8192]{1,0:T(8,128)}, u32[]{:S(2)}, u32[]{:S(2)}) collective-permute-start(f32[30,8192]{1,0:T(8,128)} %slice.15), channel_id=1, source_target_pairs={{0,8},{8,16},{16,24},{1,9},{9,17},{17,25},{2,10},{10,18},{18,26},{... | collective-permute-start | bytes 2949128
  221.5 45.5 %collective-permute-start = (bf16[64,8192]{1,0:T(8,128)(2,1)}, bf16[64,8192]{1,0:T(8,128)(2,1)}, u32[]{:S(2)}, u32[]{:S(2)}) collective-permute-start(bf16[64,8192]{1,0:T(8,128)(2,1)} %bitcast.39), channel_id=1, source_target_pairs={{8,0},{16,8},{24,16},{9,1},{17,9},{25,17},{10,2},{18,10},{26,18},{... | collective-permute-start | bytes 3145736 | tf_op jit(solution)/shard_map/ppermute | solution.py:10
  254.8 12.2 %copy-start = (f32[126,8192]{1,0:T(8,128)S(1)}, f32[126,8192]{1,0:T(8,128)}, u32[]{:S(2)}) copy-start(f32[126,8192]{1,0:T(8,128)} %concatenate.19) | copy-start | bytes 12386308
  254.8 12.2 %copy-start.14 = (bf16[1,64,8192]{2,1,0:T(8,128)(2,1)S(1)}, bf16[1,64,8192]{2,1,0:T(8,128)(2,1)}, u32[]{:S(2)}) copy-start(bf16[1,64,8192]{2,1,0:T(8,128)(2,1)} %param.9) | copy-start | bytes 3145732
  345.1 2.2 slice-start
  349.6 4.7 copy-start.3
  349.6 166.8 %all-to-all-start = ((bf16[256,8,1024]{2,0,1:T(8,128)(2,1)}), bf16[256,8,1024]{2,0,1:T(8,128)(2,1)}, u32[]{:S(2)}, u32[]{:S(2)}) async-start(bf16[256,8,1024]{2,0,1:T(8,128)(2,1)} %bitcast.38), calls=%async_computation | async-start | bytes 8388608 | tf_op jit(solution)/shard_map/all_to_all | solution.py:57
  354.4 78.2 %collective-permute-start.2 = (bf16[1024,256]{1,0:T(8,128)(2,1)S(1)}, bf16[1024,256]{1,0:T(8,128)(2,1)S(1)}, u32[]{:S(2)}, u32[]{:S(2)}) collective-permute-start(bf16[1024,256]{1,0:T(8,128)(2,1)S(1)} %copy-done.3), channel_id=1, source_target_pairs={{0,1},{1,2},{2,3},{3,4},{4,5},{5,6},{6,7},{7,0},{8,9},{9,10},{10,1... | collective-permute-start | bytes 1572872 | tf_op jit(solution)/shard_map/ppermute | solution.py:60
  432.6 0.8 copy-start.4
  433.4 10.5 %collective-permute-start.3 = (bf16[1024,256]{1,0:T(8,128)(2,1)S(1)}, bf16[1024,256]{1,0:T(8,128)(2,1)S(1)}, u32[]{:S(2)}, u32[]{:S(2)}) collective-permute-start(bf16[1024,256]{1,0:T(8,128)(2,1)S(1)} %collective-permute-done.2), channel_id=1, source_target_pairs={{0,1},{1,2},{2,3},{3,4},{4,5},{5,6},{6,7},{7,0},{8,9},{9,10},{10,1... | collective-permute-start | bytes 1572872 | tf_op jit(solution)/shard_map/ppermute | solution.py:60
  443.9 0.8 copy-start.6
  444.7 10.5 %collective-permute-start.4 = (bf16[1024,256]{1,0:T(8,128)(2,1)S(1)}, bf16[1024,256]{1,0:T(8,128)(2,1)S(1)}, u32[]{:S(2)}, u32[]{:S(2)}) collective-permute-start(bf16[1024,256]{1,0:T(8,128)(2,1)S(1)} %collective-permute-done.3), channel_id=1, source_target_pairs={{0,1},{1,2},{2,3},{3,4},{4,5},{5,6},{6,7},{7,0},{8,9},{9,10},{10,1... | collective-permute-start | bytes 1572872 | tf_op jit(solution)/shard_map/ppermute | solution.py:60
  455.2 0.8 copy-start.8
  456.0 10.5 %collective-permute-start.5 = (bf16[1024,256]{1,0:T(8,128)(2,1)S(1)}, bf16[1024,256]{1,0:T(8,128)(2,1)S(1)}, u32[]{:S(2)}, u32[]{:S(2)}) collective-permute-start(bf16[1024,256]{1,0:T(8,128)(2,1)S(1)} %collective-permute-done.4), channel_id=1, source_target_pairs={{0,1},{1,2},{2,3},{3,4},{4,5},{5,6},{6,7},{7,0},{8,9},{9,10},{10,1... | collective-permute-start | bytes 1572872 | tf_op jit(solution)/shard_map/ppermute | solution.py:60
  466.5 0.8 copy-start.10
  467.3 10.4 %collective-permute-start.6 = (bf16[1024,256]{1,0:T(8,128)(2,1)S(1)}, bf16[1024,256]{1,0:T(8,128)(2,1)S(1)}, u32[]{:S(2)}, u32[]{:S(2)}) collective-permute-start(bf16[1024,256]{1,0:T(8,128)(2,1)S(1)} %collective-permute-done.5), channel_id=1, source_target_pairs={{0,1},{1,2},{2,3},{3,4},{4,5},{5,6},{6,7},{7,0},{8,9},{9,10},{10,1... | collective-permute-start | bytes 1572872 | tf_op jit(solution)/shard_map/ppermute | solution.py:60
  477.7 0.8 copy-start.12
  478.5 10.5 %collective-permute-start.7 = (bf16[1024,256]{1,0:T(8,128)(2,1)S(1)}, bf16[1024,256]{1,0:T(8,128)(2,1)}, u32[]{:S(2)}, u32[]{:S(2)}) collective-permute-start(bf16[1024,256]{1,0:T(8,128)(2,1)S(1)} %collective-permute-done.6), channel_id=1, source_target_pairs={{0,1},{1,2},{2,3},{3,4},{4,5},{5,6},{6,7},{7,0},{8,9},{9,10},{10,1... | collective-permute-start | bytes 1572872 | tf_op jit(solution)/shard_map/ppermute | solution.py:60
  489.0 10.7 %collective-permute-start.8 = (bf16[1024,256]{1,0:T(8,128)(2,1)}, bf16[1024,256]{1,0:T(8,128)(2,1)}, u32[]{:S(2)}, u32[]{:S(2)}) collective-permute-start(bf16[1024,256]{1,0:T(8,128)(2,1)} %collective-permute-done.7), channel_id=1, source_target_pairs={{0,1},{1,2},{2,3},{3,4},{4,5},{5,6},{6,7},{7,0},{8,9},{9,10},{10,1... | collective-permute-start | bytes 1572872 | tf_op jit(solution)/shard_map/ppermute | solution.py:60
  490.1 14.2 %copy-start.9 = (bf16[1024,256]{1,0:T(8,128)(2,1)S(1)}, bf16[1024,256]{1,0:T(8,128)(2,1)}, u32[]{:S(2)}) copy-start(bf16[1024,256]{1,0:T(8,128)(2,1)} %copy-done.8) | copy-start | bytes 1572868
  490.1 14.2 %copy-start.7 = (bf16[1024,256]{1,0:T(8,128)(2,1)S(1)}, bf16[1024,256]{1,0:T(8,128)(2,1)}, u32[]{:S(2)}) copy-start(bf16[1024,256]{1,0:T(8,128)(2,1)} %copy-done.6) | copy-start | bytes 1572868
  490.1 14.3 %copy-start.5 = (bf16[1024,256]{1,0:T(8,128)(2,1)S(1)}, bf16[1024,256]{1,0:T(8,128)(2,1)}, u32[]{:S(2)}) copy-start(bf16[1024,256]{1,0:T(8,128)(2,1)} %copy-done.4) | copy-start | bytes 1572868
  501.9 5.1 copy-start.13
  503.1 4.0 copy-start.11
  504.6 2.9 copy-start.1
  507.4 4.5 copy-start.16
Sparse Core Ops, SparseCore 0:
  273.0 65.1 all-gather.2
